TPU v7x, 512 devices: a whole 4x4x16 slice. The times are simulated.
512 devices in a mesh: ctx: 16 (over z_lo, core), exp: 32 (over z_hi, x, y).
Axes of the slice: x: 4, y: 4, z: 16 (z_hi: 2, z_lo: 8; z = z_hi * 8 + z_lo), core: 2. Of those that a mesh axis runs over, the one named last changes fastest.
Arguments:
- query: bfloat16 [32, 2048, 4096], P('exp', 'ctx'), may hold values from -41 to 41
- keyval: bfloat16 [32, 2, 2048, 256], P('exp', None, 'ctx'), may hold values from -4 to 4
- doc_ids: int32 [32, 2048], P('exp', 'ctx'), may hold values from 0 to 5, never falling along the last dimension, each value on 1 to 1024 neighbouring positions
- route_ids: int32 [32, 2048], P('exp', 'ctx'), may hold values from 0 to 63
- combine: float32 [32, 2048], P('exp', 'ctx'), may hold values from 0.5 to 2
- w_gate_up: bfloat16 [32, 2, 1536, 4096], P('exp', None, 'ctx'), may hold values from -0.09375 to 0.09375
- w_down: bfloat16 [32, 1536, 4096], P('exp', None, 'ctx'), may hold values from -0.15625 to 0.15625
Outputs:
- layer_out: bfloat16 [32, 2048, 4096], P('exp', 'ctx')
All inputs are finite; a program needn't handle non-finite values.
Results may differ from a plain program's by a relative error of at most 0.024.
Values may be sent and summed in bfloat16 or wider, within the bound.
A program may use at most 128 MiB of HBM per device.

v0:
```python
import jax
import jax.numpy as jnp
from jax import lax
from jax.sharding import PartitionSpec as P

HD = 128
CAP = 2
neg_large = -1e30
norm_eps = 1e-06


def shifted(value, axis, by):
    length = lax.axis_size(axis)
    return lax.ppermute(value, axis, [(i, (i + by) % length) for i in range(length)])


def shards(query, keyval, doc_ids, route_ids, combine, w_gate_up, w_down):
    tok_rows = query.shape[1]
    feature_width = query.shape[2]
    kv_heads = keyval.shape[3] // HD
    head_group = feature_width // HD // kv_heads
    ctx_count = lax.axis_size("ctx")
    q_heads = query[0].reshape(tok_rows, kv_heads, head_group, HD)
    q_doc = doc_ids[0]
    score_scale = HD ** (-0.5)

    def attend(loop_carry, kv_pair):
        kv_piece, doc_piece = kv_pair
        rows_here = kv_piece.shape[2]
        key_rows = kv_piece[0, 0].reshape(rows_here, kv_heads, HD)
        value_rows = kv_piece[0, 1].reshape(rows_here, kv_heads, HD)
        allowed = doc_piece[0, 0][None, :] == q_doc[:, None]
        running_max, running_sum, running_out = loop_carry
        scores = (
            jnp.einsum("qhgd,khd->hgqk", q_heads, key_rows, preferred_element_type=jnp.float32)
            * score_scale
        )
        masked = jnp.where(allowed, scores, neg_large)
        fresh_max = jnp.maximum(running_max, jnp.max(masked, axis=-1))
        prob_block = jnp.where(allowed, jnp.exp(masked - fresh_max[..., None]), 0.0)
        rescale = jnp.exp(running_max - fresh_max)
        running_sum = running_sum * rescale + jnp.sum(prob_block, axis=-1)
        block_out = jnp.einsum(
            "hgqk,khd->hgqd",
            prob_block.astype(jnp.bfloat16),
            value_rows,
            preferred_element_type=jnp.float32,
        )
        return (fresh_max, running_sum, running_out * rescale[..., None] + block_out)

    start_state = (
        jnp.full((kv_heads, head_group, tok_rows), neg_large, jnp.float32),
        jnp.zeros((kv_heads, head_group, tok_rows), jnp.float32),
        jnp.zeros((kv_heads, head_group, tok_rows, HD), jnp.float32),
    )
    doc_keys = doc_ids.reshape(1, 1, tok_rows)

    def cycle_step(step_index, loop_state):
        loop_carry, kv_now, doc_now = loop_state
        loop_carry = attend(loop_carry, (kv_now, doc_now))
        kv_next, doc_next = shifted((kv_now, doc_now), "ctx", 1)
        return (loop_carry, kv_next, doc_next)

    loop_carry, kv_last, doc_last = lax.fori_loop(
        0, ctx_count - 1, cycle_step, (start_state, keyval, doc_keys)
    )
    running_max, running_sum, running_out = attend(loop_carry, (kv_last, doc_last))
    head_major = (running_out / running_sum[..., None]).astype(jnp.bfloat16)
    attended = head_major.transpose(2, 0, 1, 3).reshape(tok_rows, feature_width)
    flat_attended = attended.astype(jnp.float32)
    normed = (
        flat_attended
        * lax.rsqrt(jnp.mean(flat_attended * flat_attended, axis=-1, keepdims=True) + norm_eps)
    ).astype(jnp.bfloat16)
    expert_count = lax.axis_size("exp")
    token_ids = route_ids[0]
    onehot = (token_ids[:, None] == lax.iota(jnp.int32, expert_count)[None, :]).astype(jnp.int32)
    earlier = jnp.sum((jnp.cumsum(onehot, axis=0) - onehot) * onehot, axis=1)
    kept = (token_ids < expert_count) & (earlier < CAP)
    slot = jnp.where(kept, token_ids * CAP + earlier, -1)
    chooser = (lax.iota(jnp.int32, expert_count * CAP)[:, None] == slot[None, :]).astype(
        jnp.bfloat16
    )
    outgoing = jnp.dot(chooser, normed, preferred_element_type=jnp.float32).astype(jnp.bfloat16)
    outgoing = outgoing.reshape(expert_count, CAP, feature_width)
    arrived = lax.all_to_all(outgoing, "exp", split_axis=0, concat_axis=0, tiled=True)
    hidden_local = w_gate_up.shape[2]
    gate_up = w_gate_up[0].reshape(2 * hidden_local, feature_width)
    row_piece = lax.all_gather(arrived[None], "ctx", axis=0, tiled=True)
    piece_count = row_piece.shape[0]
    rows_flat = row_piece.reshape(-1, feature_width)
    both_parts = lax.dot_general(
        rows_flat, gate_up, (((1,), (1,)), ((), ())), preferred_element_type=jnp.float32
    )
    activation = (jax.nn.silu(both_parts[:, :hidden_local]) * both_parts[:, hidden_local:]).astype(
        jnp.bfloat16
    )
    hidden = activation.reshape(piece_count, expert_count, CAP, hidden_local)
    down_cols = w_down[0]
    column_width = down_cols.shape[1]
    hidden_piece = lax.all_gather(hidden, "ctx", axis=3, tiled=True)
    unit_count = hidden_piece.shape[3]
    made_cols = jnp.dot(
        hidden_piece.reshape(-1, unit_count), down_cols, preferred_element_type=jnp.float32
    )
    made_cols = made_cols.astype(jnp.bfloat16).reshape(ctx_count, expert_count, CAP, column_width)
    returned = lax.all_to_all(
        lax.all_to_all(made_cols, "ctx", split_axis=0, concat_axis=3, tiled=True),
        "exp",
        split_axis=1,
        concat_axis=0,
        tiled=True,
    )
    returned = returned.reshape(expert_count * CAP, feature_width)
    picked = lax.dot_general(
        chooser, returned, (((0,), (0,)), ((), ())), preferred_element_type=jnp.float32
    )
    layer_out = (flat_attended + combine[0][:, None] * picked).astype(jnp.bfloat16)
    return layer_out[None]


def solution(mesh):
    placed = (
        P("exp", "ctx", None),
        P("exp", None, "ctx", None),
        P("exp", "ctx"),
        P("exp", "ctx"),
        P("exp", "ctx"),
        P("exp", None, "ctx", None),
        P("exp", None, "ctx"),
    )
    return jax.shard_map(
        shards, mesh=mesh, in_specs=placed, out_specs=P("exp", "ctx", None), check_vma=False
    )
```

profile of v0, /device:TPU:33, one launch (start us, length us, event | category | flops | bytes accessed | tf_op | source)
XLA Modules:
  0.0 687.9 jit_solution(2477227029983482087)
XLA Ops:
  10.8 2.3 copy.43
  14.7 200.1 %while.19 = (s32[]{:T(128)}, f32[2,16,128]{2,1,0:T(8,128)S(1)}, f32[2,16,128]{2,1,0:T(8,128)S(1)}, f32[2,16,128,128]{3,2,1,0:T(8,128)}, bf16[1,2,128,256]{2,3,1,...) while((s32[]{:T(128)}, f32[2,16,128]{2,1,0:T(8,128)S(1)}, ...), condition=%wide.region_3.4_spmd.clone, body=%wide.region_0.3_spmd.clone.sunk | while | flops 276860928 | bytes 29823224 | solution.py:64
  14.7 4.1 collective-permute-start.1
  25.4 3.9 collective-permute-start.1
  35.8 5.1 collective-permute-start.1
  47.5 3.9 collective-permute-start.1
  58.0 3.9 collective-permute-start.1
  68.5 3.9 collective-permute-start.1
  79.1 2.2 collective-permute-done
  81.3 2.4 collective-permute-start.1
  90.3 3.7 collective-permute-done.1
  94.0 2.2 collective-permute-done
  96.1 2.4 collective-permute-start.1
  105.1 3.7 collective-permute-done.1
  108.8 2.2 collective-permute-done
  111.0 2.4 collective-permute-start.1
  119.9 3.7 collective-permute-done.1
  123.6 2.2 collective-permute-done
  125.8 2.4 collective-permute-start.1
  134.8 3.7 collective-permute-done.1
  140.6 2.4 collective-permute-start.1
  149.6 3.7 collective-permute-done.1
  153.3 2.2 collective-permute-done
  155.5 2.4 collective-permute-start.1
  164.4 3.7 collective-permute-done.1
  168.1 2.2 collective-permute-done
  170.3 2.4 collective-permute-start.1
  179.2 3.7 collective-permute-done.1
  182.9 2.2 collective-permute-done
  185.1 2.4 collective-permute-start.1
  194.1 3.7 collective-permute-done.1
  197.8 2.2 collective-permute-done
  199.9 2.4 collective-permute-start.1
  208.9 3.7 collective-permute-done.1
  214.8 3.0 copy.48
  222.5 32.7 %all_to_all.32 = bf16[32,2,4096]{2,1,0:T(2,128)(2,1)} all-to-all(bf16[32,2,4096]{2,1,0:T(2,128)(2,1)S(1)} %reshape.55), channel_id=1, replica_groups=mesh['ctx'=16,'exp'=32] {'exp'}, dimensions={0} | all-to-all | bytes 1048576 | tf_op jit(solution)/shard_map/all_to_all | solution.py:86
  255.5 125.6 %all-gather.6.cloned.1.call-done = bf16[512,2,4096]{2,1,0:T(2,128)(2,1)} async-done(((bf16[32,2,4096]{2,1,0:T(2,128)(2,1)}), bf16[512,2,4096]{2,1,0:T(2,128)(2,1)}) %all-gather.6.cloned.1.call-update) | async-done | bytes 8388624 | tf_op jit(solution)/shard_map/all_gather | solution.py:89
  381.1 13.1 %reshape.56 = bf16[1024,4096]{1,0:T(8,128)(2,1)} reshape(bf16[512,2,4096]{2,1,0:T(2,128)(2,1)} %all-gather.6.cloned.1.call-done) | data formatting | bytes 16777216 | tf_op jit(solution)/shard_map/reshape | solution.py:91
  394.2 6.3 fusion.39
  402.2 149.4 %all-gather.4.cloned.1.call-done = bf16[16,32,2,1536]{1,0,2,3:T(8,128)(2,1)} async-done(((bf16[16,32,2,96]{1,0,2,3:T(8,128)(2,1)}), bf16[16,32,2,1536]{1,0,2,3:T(8,128)(2,1)}) %all-gather.4.cloned.1.call-update) | async-done | bytes 3145744 | tf_op jit(solution)/shard_map/all_gather | solution.py:101
  551.6 20.2 %copy.52 = bf16[16,32,2,1536]{3,2,1,0:T(2,128)(2,1)} copy(bf16[16,32,2,1536]{1,0,2,3:T(8,128)(2,1)} %all-gather.4.cloned.1.call-done) | data formatting | bytes 6291456 | tf_op jit(solution)/shard_map/all_gather | solution.py:101
  571.8 7.5 %reshape.58 = bf16[1024,1536]{1,0:T(8,128)(2,1)} reshape(bf16[16,32,2,1536]{3,2,1,0:T(2,128)(2,1)} %copy.52) | data formatting | bytes 6291456 | tf_op jit(solution)/shard_map/reshape | solution.py:104
  579.3 3.1 convolution_convert_fusion.1
  582.7 43.1 %all_to_all.33 = bf16[16,32,2,256]{3,1,2,0:T(8,128)(2,1)S(1)} all-to-all(bf16[16,32,2,256]{3,1,2,0:T(8,128)(2,1)S(1)} %copy.53), channel_id=1, replica_groups=mesh['ctx'=16,'exp'=32] {'ctx'}, dimensions={0} | all-to-all | bytes 1048576 | tf_op jit(solution)/shard_map/all_to_all | solution.py:108
  627.0 14.2 %all-to-all-start.2 = ((bf16[1,32,2,4096]{3,2,0,1:T(2,128)(2,1)}), bf16[1,32,2,4096]{3,2,0,1:T(2,128)(2,1)S(1)}, u32[]{:S(2)}, u32[]{:S(2)}) async-start(bf16[1,32,2,4096]{3,2,0,1:T(2,128)(2,1)} %reshape.68), calls=%async_computation.2 | async-start | bytes 1048576 | tf_op jit(solution)/shard_map/all_to_all | solution.py:107
  641.3 2.9 copy.56
  644.2 33.6 %all-to-all-done.2 = bf16[1,32,2,4096]{3,2,0,1:T(2,128)(2,1)S(1)} async-done(((bf16[1,32,2,4096]{3,2,0,1:T(2,128)(2,1)}), bf16[1,32,2,4096]{3,2,0,1:T(2,128)(2,1)S(1)}, u32[]{:S(2)}, u32[]{:S(2)}) %all-to-all-start.2) | async-done | bytes 524320 | tf_op jit(solution)/shard_map/all_to_all | solution.py:107
  678.0 3.0 fusion.16
  (282 shorter events, 115.2 us)
Async XLA Ops:
  6.5 387.6 %copy-start = (bf16[1,2,96,4096]{3,2,1,0:T(8,128)(2,1)S(1)}, bf16[1,2,96,4096]{3,2,1,0:T(8,128)(2,1)}, u32[]{:S(2)}) copy-start(bf16[1,2,96,4096]{3,2,1,0:T(8,128)(2,1)} %param.14) | copy-start | bytes 4718596
  6.5 374.5 %all-gather.6.cloned.1.call-start = ((), (), s32[]{:S(2)}) async-start(), calls=%async_computation.4 | async-start | bytes 8912896 | tf_op jit(solution)/shard_map/all_gather | solution.py:89
  10.8 3.9 copy-start.6
  14.7 10.6 %collective-permute-start.1 = (s32[1,1,128]{2,1,0:T(1,128)S(1)}, s32[1,1,128]{2,1,0:T(1,128)S(1)}, u32[]{:S(2)}, u32[]{:S(2)}) collective-permute-start(s32[1,1,128]{2,1,0:T(1,128)S(1)} %copy.83), channel_id=1, source_target_pairs={{0,32},{32,64},{64,96},{96,128},{128,160},{160,192},{192,224},{224... | collective-permute-start | bytes 1544 | tf_op jit(solution)/shard_map/while/body/eval_jaxpr/ppermute | solution.py:14
  18.8 6.5 collective-permute-start
  20.9 1.6 copy-start.1
  25.4 10.5 %collective-permute-start.1 = (s32[1,1,128]{2,1,0:T(1,128)S(1)}, s32[1,1,128]{2,1,0:T(1,128)S(1)}, u32[]{:S(2)}, u32[]{:S(2)}) collective-permute-start(s32[1,1,128]{2,1,0:T(1,128)S(1)} %copy.83), channel_id=1, source_target_pairs={{0,32},{32,64},{64,96},{96,128},{128,160},{160,192},{192,224},{224... | collective-permute-start | bytes 1544 | tf_op jit(solution)/shard_map/while/body/eval_jaxpr/ppermute | solution.py:14
  29.3 6.5 collective-permute-start
  31.4 1.6 copy-start.1
  35.8 11.7 %collective-permute-start.1 = (s32[1,1,128]{2,1,0:T(1,128)S(1)}, s32[1,1,128]{2,1,0:T(1,128)S(1)}, u32[]{:S(2)}, u32[]{:S(2)}) collective-permute-start(s32[1,1,128]{2,1,0:T(1,128)S(1)} %copy.83), channel_id=1, source_target_pairs={{0,32},{32,64},{64,96},{96,128},{128,160},{160,192},{192,224},{224... | collective-permute-start | bytes 1544 | tf_op jit(solution)/shard_map/while/body/eval_jaxpr/ppermute | solution.py:14
  41.0 6.5 collective-permute-start
  43.0 1.6 copy-start.1
  47.5 10.5 %collective-permute-start.1 = (s32[1,1,128]{2,1,0:T(1,128)S(1)}, s32[1,1,128]{2,1,0:T(1,128)S(1)}, u32[]{:S(2)}, u32[]{:S(2)}) collective-permute-start(s32[1,1,128]{2,1,0:T(1,128)S(1)} %copy.83), channel_id=1, source_target_pairs={{0,32},{32,64},{64,96},{96,128},{128,160},{160,192},{192,224},{224... | collective-permute-start | bytes 1544 | tf_op jit(solution)/shard_map/while/body/eval_jaxpr/ppermute | solution.py:14
  51.5 6.5 collective-permute-start
  53.5 1.6 copy-start.1
  58.0 10.5 %collective-permute-start.1 = (s32[1,1,128]{2,1,0:T(1,128)S(1)}, s32[1,1,128]{2,1,0:T(1,128)S(1)}, u32[]{:S(2)}, u32[]{:S(2)}) collective-permute-start(s32[1,1,128]{2,1,0:T(1,128)S(1)} %copy.83), channel_id=1, source_target_pairs={{0,32},{32,64},{64,96},{96,128},{128,160},{160,192},{192,224},{224... | collective-permute-start | bytes 1544 | tf_op jit(solution)/shard_map/while/body/eval_jaxpr/ppermute | solution.py:14
  62.0 6.5 collective-permute-start
  64.0 1.6 copy-start.1
  68.5 10.6 %collective-permute-start.1 = (s32[1,1,128]{2,1,0:T(1,128)S(1)}, s32[1,1,128]{2,1,0:T(1,128)S(1)}, u32[]{:S(2)}, u32[]{:S(2)}) collective-permute-start(s32[1,1,128]{2,1,0:T(1,128)S(1)} %copy.83), channel_id=1, source_target_pairs={{0,32},{32,64},{64,96},{96,128},{128,160},{160,192},{192,224},{224... | collective-permute-start | bytes 1544 | tf_op jit(solution)/shard_map/while/body/eval_jaxpr/ppermute | solution.py:14
  72.5 8.9 %collective-permute-start = (bf16[1,2,128,256]{2,3,1,0:T(8,128)(2,1)S(1)}, bf16[1,2,128,256]{2,3,1,0:T(8,128)(2,1)S(1)}, u32[]{:S(2)}, u32[]{:S(2)}) collective-permute-start(bf16[1,2,128,256]{2,3,1,0:T(8,128)(2,1)S(1)} %copy.82), channel_id=1, source_target_pairs={{0,32},{32,64},{64,96},{96,128},{128,160},{160,192},{192,224},{224... | collective-permute-start | bytes 393224 | tf_op jit(solution)/shard_map/while/body/eval_jaxpr/ppermute | solution.py:14
  74.5 1.6 copy-start.1
  81.3 12.7 %collective-permute-start.1 = (s32[1,1,128]{2,1,0:T(1,128)S(1)}, s32[1,1,128]{2,1,0:T(1,128)S(1)}, u32[]{:S(2)}, u32[]{:S(2)}) collective-permute-start(s32[1,1,128]{2,1,0:T(1,128)S(1)} %copy.83), channel_id=1, source_target_pairs={{0,32},{32,64},{64,96},{96,128},{128,160},{160,192},{192,224},{224... | collective-permute-start | bytes 1544 | tf_op jit(solution)/shard_map/while/body/eval_jaxpr/ppermute | solution.py:14
  83.8 12.4 %collective-permute-start = (bf16[1,2,128,256]{2,3,1,0:T(8,128)(2,1)S(1)}, bf16[1,2,128,256]{2,3,1,0:T(8,128)(2,1)S(1)}, u32[]{:S(2)}, u32[]{:S(2)}) collective-permute-start(bf16[1,2,128,256]{2,3,1,0:T(8,128)(2,1)S(1)} %copy.82), channel_id=1, source_target_pairs={{0,32},{32,64},{64,96},{96,128},{128,160},{160,192},{192,224},{224... | collective-permute-start | bytes 393224 | tf_op jit(solution)/shard_map/while/body/eval_jaxpr/ppermute | solution.py:14
  85.8 1.6 copy-start.1
  96.1 12.7 %collective-permute-start.1 = (s32[1,1,128]{2,1,0:T(1,128)S(1)}, s32[1,1,128]{2,1,0:T(1,128)S(1)}, u32[]{:S(2)}, u32[]{:S(2)}) collective-permute-start(s32[1,1,128]{2,1,0:T(1,128)S(1)} %copy.83), channel_id=1, source_target_pairs={{0,32},{32,64},{64,96},{96,128},{128,160},{160,192},{192,224},{224... | collective-permute-start | bytes 1544 | tf_op jit(solution)/shard_map/while/body/eval_jaxpr/ppermute | solution.py:14
  98.6 12.4 %collective-permute-start = (bf16[1,2,128,256]{2,3,1,0:T(8,128)(2,1)S(1)}, bf16[1,2,128,256]{2,3,1,0:T(8,128)(2,1)S(1)}, u32[]{:S(2)}, u32[]{:S(2)}) collective-permute-start(bf16[1,2,128,256]{2,3,1,0:T(8,128)(2,1)S(1)} %copy.82), channel_id=1, source_target_pairs={{0,32},{32,64},{64,96},{96,128},{128,160},{160,192},{192,224},{224... | collective-permute-start | bytes 393224 | tf_op jit(solution)/shard_map/while/body/eval_jaxpr/ppermute | solution.py:14
  100.7 1.6 copy-start.1
  111.0 12.7 %collective-permute-start.1 = (s32[1,1,128]{2,1,0:T(1,128)S(1)}, s32[1,1,128]{2,1,0:T(1,128)S(1)}, u32[]{:S(2)}, u32[]{:S(2)}) collective-permute-start(s32[1,1,128]{2,1,0:T(1,128)S(1)} %copy.83), channel_id=1, source_target_pairs={{0,32},{32,64},{64,96},{96,128},{128,160},{160,192},{192,224},{224... | collective-permute-start | bytes 1544 | tf_op jit(solution)/shard_map/while/body/eval_jaxpr/ppermute | solution.py:14
  113.4 12.4 %collective-permute-start = (bf16[1,2,128,256]{2,3,1,0:T(8,128)(2,1)S(1)}, bf16[1,2,128,256]{2,3,1,0:T(8,128)(2,1)S(1)}, u32[]{:S(2)}, u32[]{:S(2)}) collective-permute-start(bf16[1,2,128,256]{2,3,1,0:T(8,128)(2,1)S(1)} %copy.82), channel_id=1, source_target_pairs={{0,32},{32,64},{64,96},{96,128},{128,160},{160,192},{192,224},{224... | collective-permute-start | bytes 393224 | tf_op jit(solution)/shard_map/while/body/eval_jaxpr/ppermute | solution.py:14
  115.5 1.6 copy-start.1
  125.8 12.7 %collective-permute-start.1 = (s32[1,1,128]{2,1,0:T(1,128)S(1)}, s32[1,1,128]{2,1,0:T(1,128)S(1)}, u32[]{:S(2)}, u32[]{:S(2)}) collective-permute-start(s32[1,1,128]{2,1,0:T(1,128)S(1)} %copy.83), channel_id=1, source_target_pairs={{0,32},{32,64},{64,96},{96,128},{128,160},{160,192},{192,224},{224... | collective-permute-start | bytes 1544 | tf_op jit(solution)/shard_map/while/body/eval_jaxpr/ppermute | solution.py:14
  128.3 12.4 %collective-permute-start = (bf16[1,2,128,256]{2,3,1,0:T(8,128)(2,1)S(1)}, bf16[1,2,128,256]{2,3,1,0:T(8,128)(2,1)S(1)}, u32[]{:S(2)}, u32[]{:S(2)}) collective-permute-start(bf16[1,2,128,256]{2,3,1,0:T(8,128)(2,1)S(1)} %copy.82), channel_id=1, source_target_pairs={{0,32},{32,64},{64,96},{96,128},{128,160},{160,192},{192,224},{224... | collective-permute-start | bytes 393224 | tf_op jit(solution)/shard_map/while/body/eval_jaxpr/ppermute | solution.py:14
  140.6 12.7 %collective-permute-start.1 = (s32[1,1,128]{2,1,0:T(1,128)S(1)}, s32[1,1,128]{2,1,0:T(1,128)S(1)}, u32[]{:S(2)}, u32[]{:S(2)}) collective-permute-start(s32[1,1,128]{2,1,0:T(1,128)S(1)} %copy.83), channel_id=1, source_target_pairs={{0,32},{32,64},{64,96},{96,128},{128,160},{160,192},{192,224},{224... | collective-permute-start | bytes 1544 | tf_op jit(solution)/shard_map/while/body/eval_jaxpr/ppermute | solution.py:14
  143.1 12.4 %collective-permute-start = (bf16[1,2,128,256]{2,3,1,0:T(8,128)(2,1)S(1)}, bf16[1,2,128,256]{2,3,1,0:T(8,128)(2,1)S(1)}, u32[]{:S(2)}, u32[]{:S(2)}) collective-permute-start(bf16[1,2,128,256]{2,3,1,0:T(8,128)(2,1)S(1)} %copy.82), channel_id=1, source_target_pairs={{0,32},{32,64},{64,96},{96,128},{128,160},{160,192},{192,224},{224... | collective-permute-start | bytes 393224 | tf_op jit(solution)/shard_map/while/body/eval_jaxpr/ppermute | solution.py:14
  155.5 12.7 %collective-permute-start.1 = (s32[1,1,128]{2,1,0:T(1,128)S(1)}, s32[1,1,128]{2,1,0:T(1,128)S(1)}, u32[]{:S(2)}, u32[]{:S(2)}) collective-permute-start(s32[1,1,128]{2,1,0:T(1,128)S(1)} %copy.83), channel_id=1, source_target_pairs={{0,32},{32,64},{64,96},{96,128},{128,160},{160,192},{192,224},{224... | collective-permute-start | bytes 1544 | tf_op jit(solution)/shard_map/while/body/eval_jaxpr/ppermute | solution.py:14
  157.9 12.4 %collective-permute-start = (bf16[1,2,128,256]{2,3,1,0:T(8,128)(2,1)S(1)}, bf16[1,2,128,256]{2,3,1,0:T(8,128)(2,1)S(1)}, u32[]{:S(2)}, u32[]{:S(2)}) collective-permute-start(bf16[1,2,128,256]{2,3,1,0:T(8,128)(2,1)S(1)} %copy.82), channel_id=1, source_target_pairs={{0,32},{32,64},{64,96},{96,128},{128,160},{160,192},{192,224},{224... | collective-permute-start | bytes 393224 | tf_op jit(solution)/shard_map/while/body/eval_jaxpr/ppermute | solution.py:14
  160.0 1.6 copy-start.1
  170.3 12.7 %collective-permute-start.1 = (s32[1,1,128]{2,1,0:T(1,128)S(1)}, s32[1,1,128]{2,1,0:T(1,128)S(1)}, u32[]{:S(2)}, u32[]{:S(2)}) collective-permute-start(s32[1,1,128]{2,1,0:T(1,128)S(1)} %copy.83), channel_id=1, source_target_pairs={{0,32},{32,64},{64,96},{96,128},{128,160},{160,192},{192,224},{224... | collective-permute-start | bytes 1544 | tf_op jit(solution)/shard_map/while/body/eval_jaxpr/ppermute | solution.py:14
  172.8 12.4 %collective-permute-start = (bf16[1,2,128,256]{2,3,1,0:T(8,128)(2,1)S(1)}, bf16[1,2,128,256]{2,3,1,0:T(8,128)(2,1)S(1)}, u32[]{:S(2)}, u32[]{:S(2)}) collective-permute-start(bf16[1,2,128,256]{2,3,1,0:T(8,128)(2,1)S(1)} %copy.82), channel_id=1, source_target_pairs={{0,32},{32,64},{64,96},{96,128},{128,160},{160,192},{192,224},{224... | collective-permute-start | bytes 393224 | tf_op jit(solution)/shard_map/while/body/eval_jaxpr/ppermute | solution.py:14
  185.1 12.7 %collective-permute-start.1 = (s32[1,1,128]{2,1,0:T(1,128)S(1)}, s32[1,1,128]{2,1,0:T(1,128)S(1)}, u32[]{:S(2)}, u32[]{:S(2)}) collective-permute-start(s32[1,1,128]{2,1,0:T(1,128)S(1)} %copy.83), channel_id=1, source_target_pairs={{0,32},{32,64},{64,96},{96,128},{128,160},{160,192},{192,224},{224... | collective-permute-start | bytes 1544 | tf_op jit(solution)/shard_map/while/body/eval_jaxpr/ppermute | solution.py:14
  187.6 12.4 %collective-permute-start = (bf16[1,2,128,256]{2,3,1,0:T(8,128)(2,1)S(1)}, bf16[1,2,128,256]{2,3,1,0:T(8,128)(2,1)S(1)}, u32[]{:S(2)}, u32[]{:S(2)}) collective-permute-start(bf16[1,2,128,256]{2,3,1,0:T(8,128)(2,1)S(1)} %copy.82), channel_id=1, source_target_pairs={{0,32},{32,64},{64,96},{96,128},{128,160},{160,192},{192,224},{224... | collective-permute-start | bytes 393224 | tf_op jit(solution)/shard_map/while/body/eval_jaxpr/ppermute | solution.py:14
  189.6 1.6 copy-start.1
  199.9 12.7 %collective-permute-start.1 = (s32[1,1,128]{2,1,0:T(1,128)S(1)}, s32[1,1,128]{2,1,0:T(1,128)S(1)}, u32[]{:S(2)}, u32[]{:S(2)}) collective-permute-start(s32[1,1,128]{2,1,0:T(1,128)S(1)} %copy.83), channel_id=1, source_target_pairs={{0,32},{32,64},{64,96},{96,128},{128,160},{160,192},{192,224},{224... | collective-permute-start | bytes 1544 | tf_op jit(solution)/shard_map/while/body/eval_jaxpr/ppermute | solution.py:14
  202.4 12.4 %collective-permute-start = (bf16[1,2,128,256]{2,3,1,0:T(8,128)(2,1)S(1)}, bf16[1,2,128,256]{2,3,1,0:T(8,128)(2,1)S(1)}, u32[]{:S(2)}, u32[]{:S(2)}) collective-permute-start(bf16[1,2,128,256]{2,3,1,0:T(8,128)(2,1)S(1)} %copy.82), channel_id=1, source_target_pairs={{0,32},{32,64},{64,96},{96,128},{128,160},{160,192},{192,224},{224... | collective-permute-start | bytes 393224 | tf_op jit(solution)/shard_map/while/body/eval_jaxpr/ppermute | solution.py:14
  214.8 3.1 copy-start.3
  255.3 296.3 %all-gather.4.cloned.1.call-start = ((), (), s32[]{:S(2)}) async-start(), calls=%async_computation.3 | async-start | bytes 13369344 | tf_op jit(solution)/shard_map/all_gather | solution.py:101
  627.0 50.7 %all-to-all-start.2 = ((bf16[1,32,2,4096]{3,2,0,1:T(2,128)(2,1)}), bf16[1,32,2,4096]{3,2,0,1:T(2,128)(2,1)S(1)}, u32[]{:S(2)}, u32[]{:S(2)}) async-start(bf16[1,32,2,4096]{3,2,0,1:T(2,128)(2,1)} %reshape.68), calls=%async_computation.2 | async-start | bytes 1048576 | tf_op jit(solution)/shard_map/all_to_all | solution.py:107
  641.3 36.7 %copy-start.7 = (f32[1,128]{1,0:T(1,128)S(1)}, f32[1,128]{1,0:T(1,128)}, u32[]{:S(2)}) copy-start(f32[1,128]{1,0:T(1,128)} %param.13) | copy-start | bytes 1540
  (21 other events, 29.4 us)
Sparse Core Ops, SparseCore 0:
  255.4 125.6 all-gather.5
  402.3 149.2 all-gather.3
where the time goes:
time: 691 us; the launch traced here: 688 us
  waiting for transfers between devices  364 us (53%)
  starting transfers between devices  90.1 us (13%)
  local copies, waits for them, and re-layouts  85.2 us (12%)
  blocking collectives  75.9 us (11%)
  matrix products  44.7 us (6%)
  between operations  13.6 us (2%)
  other arithmetic  13.1 us (2%)
    all_gather x1, waiting for transfers between devices, shards(): hidden_piece = lax.all_gather(hidden, 'ctx', axis=3, tiled=True)  149 us
    all_gather x1, waiting for transfers between devices, shards(): row_piece = lax.all_gather(arrived[None], 'ctx', axis=0, tiled=True)  126 us
    ppermute x30, starting transfers between devices, shifted(): lax.ppermute(value, axis, [(i, (i + by) % length) for i in range(length)])  75.7 us
    ppermute x30, waiting for transfers between devices, shifted(): lax.ppermute(value, axis, [(i, (i + by) % length) for i in range(length)])  55.2 us
    all_to_all x1, blocking collectives, shards(): lax.all_to_all(made_cols, 'ctx', split_axis=0, concat_axis=3, tiled=True)  43.1 us
    all_to_all x1, waiting for transfers between devices, shards(): lax.all_to_all(lax.all_to_all(made_cols, 'ctx', split_axis=0, concat_axis...  33.6 us
    all_to_all x1, blocking collectives, shards(): lax.all_to_all(outgoing, 'exp', split_axis=0, concat_axis=0, tiled=True)  32.7 us
    while x105, local copies, waits for them, and re-layouts  27.2 us
  transfers between devices with their start and end apart: 33, of which 23 were waited for; matrix products, arithmetic and copies ran while one was open for 6% of the time, Pallas kernels for 0%

commit v1 on v0

--- a/solution.py
+++ b/solution.py
@@ -86,7 +86,9 @@
     arrived = lax.all_to_all(outgoing, "exp", split_axis=0, concat_axis=0, tiled=True)
     hidden_local = w_gate_up.shape[2]
     gate_up = w_gate_up[0].reshape(2 * hidden_local, feature_width)
-    row_piece = lax.all_gather(arrived[None], "ctx", axis=0, tiled=True)
+    row_piece = jnp.concatenate(
+        lax.all_to_all(jnp.stack([arrived[None]] * lax.axis_size("ctx")), "ctx", 0, 0), axis=0
+    )
     piece_count = row_piece.shape[0]
     rows_flat = row_piece.reshape(-1, feature_width)
     both_parts = lax.dot_general(

time: 691 us -> 955 us (1.38)
  blocking collectives: 75.9 us -> 475 us
  waiting for transfers between devices: 364 us -> 222 us
    all_to_all x0 -> x1, blocking collectives: none -> 399 us  [shards(): lax.all_to_all(jnp.stack([arrived[None]] * lax.axis_size('ctx')), 'ctx',...]
    all_gather x1 -> x0, waiting for transfers between devices: 126 us -> none  [shards(): row_piece = lax.all_gather(arrived[None], 'ctx', axis=0, tiled=True)]
    another operation x0 -> x2, local copies, waits for them, and re-layouts: none -> 20.8 us  [the longest x1 13.1 us: shards(): rows_flat = row_piece.reshape(-1, feature_width)]
    all_gather x1, waiting for transfers between devices: 149 us -> 133 us  [shards(): hidden_piece = lax.all_gather(hidden, 'ctx', axis=3, tiled=True)]
    reshape x1 -> x0, local copies, waits for them, and re-layouts: 13.1 us -> none  [shards(): rows_flat = row_piece.reshape(-1, feature_width)]
  transfers between devices with their start and end apart: 33 -> 32, of which waited for: 23 -> 22; matrix products, arithmetic and copies ran while one was open for 6% -> 5% of each run, Pallas kernels for 0% -> 0%
where the time goes in v1:
time: 955 us; the launch traced here: 952 us
  blocking collectives  475 us (50%)
  waiting for transfers between devices  222 us (23%)
  local copies, waits for them, and re-layouts  92.8 us (10%)
  starting transfers between devices  89.7 us (9%)
  matrix products  44.7 us (5%)
  between operations  13.6 us (1%)
  other arithmetic  13.1 us (1%)
    all_to_all x1, blocking collectives, shards(): lax.all_to_all(jnp.stack([arrived[None]] * lax.axis_size('ctx')), 'ctx',...  399 us
    all_gather x1, waiting for transfers between devices, shards(): hidden_piece = lax.all_gather(hidden, 'ctx', axis=3, tiled=True)  133 us
    ppermute x30, starting transfers between devices, shifted(): lax.ppermute(value, axis, [(i, (i + by) % length) for i in range(length)])  75.5 us
    ppermute x30, waiting for transfers between devices, shifted(): lax.ppermute(value, axis, [(i, (i + by) % length) for i in range(length)])  55.4 us
    all_to_all x1, blocking collectives, shards(): lax.all_to_all(made_cols, 'ctx', split_axis=0, concat_axis=3, tiled=True)  43.1 us
    all_to_all x1, waiting for transfers between devices, shards(): lax.all_to_all(lax.all_to_all(made_cols, 'ctx', split_axis=0, concat_axis...  33.5 us
    all_to_all x1, blocking collectives, shards(): lax.all_to_all(outgoing, 'exp', split_axis=0, concat_axis=0, tiled=True)  32.6 us
    while x105, local copies, waits for them, and re-layouts  27.1 us
  transfers between devices with their start and end apart: 32, of which 22 were waited for; matrix products, arithmetic and copies ran while one was open for 5% of the time, Pallas kernels for 0%

profile of v1, /device:TPU:33, one launch (start us, length us, event | category | flops | bytes accessed | tf_op | source)
XLA Modules:
  0.0 952.3 jit_solution(413220307102580017)
XLA Ops:
  10.8 2.3 copy.43
  14.7 200.1 %while.19 = (s32[]{:T(128)}, f32[2,16,128]{2,1,0:T(8,128)S(1)}, f32[2,16,128]{2,1,0:T(8,128)S(1)}, f32[2,16,128,128]{3,2,1,0:T(8,128)}, bf16[1,2,128,256]{2,3,1,...) while((s32[]{:T(128)}, f32[2,16,128]{2,1,0:T(8,128)S(1)}, ...), condition=%wide.region_3.4_spmd.clone, body=%wide.region_0.3_spmd.clone.sunk | while | flops 276860928 | bytes 29823224 | solution.py:64
  14.7 4.1 collective-permute-start.1
  25.3 3.9 collective-permute-start.1
  35.8 5.1 collective-permute-start.1
  47.5 3.9 collective-permute-start.1
  58.0 3.9 collective-permute-start.1
  68.5 3.9 collective-permute-start.1
  79.1 2.2 collective-permute-done
  81.3 2.4 collective-permute-start.1
  90.3 3.7 collective-permute-done.1
  94.0 2.2 collective-permute-done
  96.1 2.4 collective-permute-start.1
  105.1 3.7 collective-permute-done.1
  108.8 2.2 collective-permute-done
  111.0 2.4 collective-permute-start.1
  119.9 3.7 collective-permute-done.1
  123.6 2.2 collective-permute-done
  125.8 2.4 collective-permute-start.1
  134.7 3.7 collective-permute-done.1
  140.6 2.4 collective-permute-start.1
  149.6 3.7 collective-permute-done.1
  153.3 2.2 collective-permute-done
  155.5 2.4 collective-permute-start.1
  164.4 3.7 collective-permute-done.1
  168.1 2.2 collective-permute-done
  170.3 2.4 collective-permute-start.1
  179.2 3.7 collective-permute-done.1
  182.9 2.2 collective-permute-done
  185.1 2.4 collective-permute-start.1
  194.1 3.7 collective-permute-done.1
  199.9 2.4 collective-permute-start.1
  208.9 3.7 collective-permute-done.1
  214.8 3.0 copy.48
  222.5 32.6 %all_to_all.37 = bf16[32,2,4096]{2,1,0:T(2,128)(2,1)S(1)} all-to-all(bf16[32,2,4096]{2,1,0:T(2,128)(2,1)S(1)} %reshape.54), channel_id=1, replica_groups=mesh['ctx'=16,'exp'=32] {'exp'}, dimensions={0} | all-to-all | bytes 1048576 | tf_op jit(solution)/shard_map/all_to_all | solution.py:86
  255.1 7.7 stack.3
  262.8 399.5 %all_to_all.38 = bf16[16,1,32,2,4096]{4,3,2,1,0:T(2,128)(2,1)} all-to-all(bf16[16,1,32,2,4096]{4,3,2,1,0:T(2,128)(2,1)S(1)} %stack.3), channel_id=1, replica_groups=mesh['ctx'=16,'exp'=32] {'ctx'}, dimensions={0} | all-to-all | bytes 16777216 | tf_op jit(solution)/shard_map/all_to_all | solution.py:90
  662.3 13.1 %reshape_reshape.3 = bf16[1024,4096]{1,0:T(8,128)(2,1)} reshape(bf16[16,1,32,2,4096]{4,3,2,1,0:T(2,128)(2,1)} %all_to_all.38) | data formatting | bytes 16777216 | tf_op jit(solution)/shard_map/reshape;reshape | solution.py:93
  675.4 6.3 fusion.39
  683.5 132.6 %all-gather.2.cloned.1.call-done = bf16[16,32,2,1536]{1,0,2,3:T(8,128)(2,1)} async-done(((bf16[16,32,2,96]{1,0,2,3:T(8,128)(2,1)}), bf16[16,32,2,1536]{1,0,2,3:T(8,128)(2,1)}) %all-gather.2.cloned.1.call-update) | async-done | bytes 3145744 | tf_op jit(solution)/shard_map/all_gather | solution.py:103
  816.1 20.2 %copy.52 = bf16[16,32,2,1536]{3,2,1,0:T(2,128)(2,1)} copy(bf16[16,32,2,1536]{1,0,2,3:T(8,128)(2,1)} %all-gather.2.cloned.1.call-done) | data formatting | bytes 6291456 | tf_op jit(solution)/shard_map/all_gather | solution.py:103
  836.3 7.5 reshape.56
  843.8 3.1 convolution_convert_fusion.1
  847.2 43.1 %all_to_all.39 = bf16[16,32,2,256]{3,1,2,0:T(8,128)(2,1)S(1)} all-to-all(bf16[16,32,2,256]{3,1,2,0:T(8,128)(2,1)S(1)} %copy.53), channel_id=1, replica_groups=mesh['ctx'=16,'exp'=32] {'ctx'}, dimensions={0} | all-to-all | bytes 1048576 | tf_op jit(solution)/shard_map/all_to_all | solution.py:110
  891.5 14.2 %all-to-all-start.3 = ((bf16[1,32,2,4096]{3,2,0,1:T(2,128)(2,1)}), bf16[1,32,2,4096]{3,2,0,1:T(2,128)(2,1)S(1)}, u32[]{:S(2)}, u32[]{:S(2)}) async-start(bf16[1,32,2,4096]{3,2,0,1:T(2,128)(2,1)} %reshape.64), calls=%async_computation.3 | async-start | bytes 1048576 | tf_op jit(solution)/shard_map/all_to_all | solution.py:109
  905.8 2.9 copy.56
  908.7 33.5 %all-to-all-done.3 = bf16[1,32,2,4096]{3,2,0,1:T(2,128)(2,1)S(1)} async-done(((bf16[1,32,2,4096]{3,2,0,1:T(2,128)(2,1)}), bf16[1,32,2,4096]{3,2,0,1:T(2,128)(2,1)S(1)}, u32[]{:S(2)}, u32[]{:S(2)}) %all-to-all-start.3) | async-done | bytes 524320 | tf_op jit(solution)/shard_map/all_to_all | solution.py:109
  942.4 3.0 fusion.16
  (281 shorter events, 117.1 us)
Async XLA Ops:
  6.5 668.9 %copy-start = (bf16[1,2,96,4096]{3,2,1,0:T(8,128)(2,1)S(1)}, bf16[1,2,96,4096]{3,2,1,0:T(8,128)(2,1)}, u32[]{:S(2)}) copy-start(bf16[1,2,96,4096]{3,2,1,0:T(8,128)(2,1)} %param.14) | copy-start | bytes 4718596
  6.5 809.6 %all-gather.2.cloned.1.call-start = ((), (), s32[]{:S(2)}) async-start(), calls=%async_computation.4 | async-start | bytes 13369344 | tf_op jit(solution)/shard_map/all_gather | solution.py:103
  10.8 3.9 copy-start.6
  14.7 10.6 %collective-permute-start.1 = (s32[1,1,128]{2,1,0:T(1,128)S(1)}, s32[1,1,128]{2,1,0:T(1,128)S(1)}, u32[]{:S(2)}, u32[]{:S(2)}) collective-permute-start(s32[1,1,128]{2,1,0:T(1,128)S(1)} %copy.83), channel_id=1, source_target_pairs={{0,32},{32,64},{64,96},{96,128},{128,160},{160,192},{192,224},{224... | collective-permute-start | bytes 1544 | tf_op jit(solution)/shard_map/while/body/eval_jaxpr/ppermute | solution.py:14
  18.8 6.5 collective-permute-start
  20.9 1.6 copy-start.1
  25.3 10.5 %collective-permute-start.1 = (s32[1,1,128]{2,1,0:T(1,128)S(1)}, s32[1,1,128]{2,1,0:T(1,128)S(1)}, u32[]{:S(2)}, u32[]{:S(2)}) collective-permute-start(s32[1,1,128]{2,1,0:T(1,128)S(1)} %copy.83), channel_id=1, source_target_pairs={{0,32},{32,64},{64,96},{96,128},{128,160},{160,192},{192,224},{224... | collective-permute-start | bytes 1544 | tf_op jit(solution)/shard_map/while/body/eval_jaxpr/ppermute | solution.py:14
  29.3 6.5 collective-permute-start
  31.3 1.6 copy-start.1
  35.8 11.7 %collective-permute-start.1 = (s32[1,1,128]{2,1,0:T(1,128)S(1)}, s32[1,1,128]{2,1,0:T(1,128)S(1)}, u32[]{:S(2)}, u32[]{:S(2)}) collective-permute-start(s32[1,1,128]{2,1,0:T(1,128)S(1)} %copy.83), channel_id=1, source_target_pairs={{0,32},{32,64},{64,96},{96,128},{128,160},{160,192},{192,224},{224... | collective-permute-start | bytes 1544 | tf_op jit(solution)/shard_map/while/body/eval_jaxpr/ppermute | solution.py:14
  41.0 6.5 collective-permute-start
  43.0 1.6 copy-start.1
  47.5 10.5 %collective-permute-start.1 = (s32[1,1,128]{2,1,0:T(1,128)S(1)}, s32[1,1,128]{2,1,0:T(1,128)S(1)}, u32[]{:S(2)}, u32[]{:S(2)}) collective-permute-start(s32[1,1,128]{2,1,0:T(1,128)S(1)} %copy.83), channel_id=1, source_target_pairs={{0,32},{32,64},{64,96},{96,128},{128,160},{160,192},{192,224},{224... | collective-permute-start | bytes 1544 | tf_op jit(solution)/shard_map/while/body/eval_jaxpr/ppermute | solution.py:14
  51.5 6.5 collective-permute-start
  53.5 1.6 copy-start.1
  58.0 10.5 %collective-permute-start.1 = (s32[1,1,128]{2,1,0:T(1,128)S(1)}, s32[1,1,128]{2,1,0:T(1,128)S(1)}, u32[]{:S(2)}, u32[]{:S(2)}) collective-permute-start(s32[1,1,128]{2,1,0:T(1,128)S(1)} %copy.83), channel_id=1, source_target_pairs={{0,32},{32,64},{64,96},{96,128},{128,160},{160,192},{192,224},{224... | collective-permute-start | bytes 1544 | tf_op jit(solution)/shard_map/while/body/eval_jaxpr/ppermute | solution.py:14
  62.0 6.5 collective-permute-start
  64.0 1.6 copy-start.1
  68.5 10.7 %collective-permute-start.1 = (s32[1,1,128]{2,1,0:T(1,128)S(1)}, s32[1,1,128]{2,1,0:T(1,128)S(1)}, u32[]{:S(2)}, u32[]{:S(2)}) collective-permute-start(s32[1,1,128]{2,1,0:T(1,128)S(1)} %copy.83), channel_id=1, source_target_pairs={{0,32},{32,64},{64,96},{96,128},{128,160},{160,192},{192,224},{224... | collective-permute-start | bytes 1544 | tf_op jit(solution)/shard_map/while/body/eval_jaxpr/ppermute | solution.py:14
  72.4 8.9 collective-permute-start
  74.5 1.6 copy-start.1
  81.3 12.7 %collective-permute-start.1 = (s32[1,1,128]{2,1,0:T(1,128)S(1)}, s32[1,1,128]{2,1,0:T(1,128)S(1)}, u32[]{:S(2)}, u32[]{:S(2)}) collective-permute-start(s32[1,1,128]{2,1,0:T(1,128)S(1)} %copy.83), channel_id=1, source_target_pairs={{0,32},{32,64},{64,96},{96,128},{128,160},{160,192},{192,224},{224... | collective-permute-start | bytes 1544 | tf_op jit(solution)/shard_map/while/body/eval_jaxpr/ppermute | solution.py:14
  83.8 12.4 %collective-permute-start = (bf16[1,2,128,256]{2,3,1,0:T(8,128)(2,1)S(1)}, bf16[1,2,128,256]{2,3,1,0:T(8,128)(2,1)S(1)}, u32[]{:S(2)}, u32[]{:S(2)}) collective-permute-start(bf16[1,2,128,256]{2,3,1,0:T(8,128)(2,1)S(1)} %copy.82), channel_id=1, source_target_pairs={{0,32},{32,64},{64,96},{96,128},{128,160},{160,192},{192,224},{224... | collective-permute-start | bytes 393224 | tf_op jit(solution)/shard_map/while/body/eval_jaxpr/ppermute | solution.py:14
  85.8 1.6 copy-start.1
  96.1 12.7 %collective-permute-start.1 = (s32[1,1,128]{2,1,0:T(1,128)S(1)}, s32[1,1,128]{2,1,0:T(1,128)S(1)}, u32[]{:S(2)}, u32[]{:S(2)}) collective-permute-start(s32[1,1,128]{2,1,0:T(1,128)S(1)} %copy.83), channel_id=1, source_target_pairs={{0,32},{32,64},{64,96},{96,128},{128,160},{160,192},{192,224},{224... | collective-permute-start | bytes 1544 | tf_op jit(solution)/shard_map/while/body/eval_jaxpr/ppermute | solution.py:14
  98.6 12.4 %collective-permute-start = (bf16[1,2,128,256]{2,3,1,0:T(8,128)(2,1)S(1)}, bf16[1,2,128,256]{2,3,1,0:T(8,128)(2,1)S(1)}, u32[]{:S(2)}, u32[]{:S(2)}) collective-permute-start(bf16[1,2,128,256]{2,3,1,0:T(8,128)(2,1)S(1)} %copy.82), channel_id=1, source_target_pairs={{0,32},{32,64},{64,96},{96,128},{128,160},{160,192},{192,224},{224... | collective-permute-start | bytes 393224 | tf_op jit(solution)/shard_map/while/body/eval_jaxpr/ppermute | solution.py:14
  100.6 1.6 copy-start.1
  111.0 12.7 %collective-permute-start.1 = (s32[1,1,128]{2,1,0:T(1,128)S(1)}, s32[1,1,128]{2,1,0:T(1,128)S(1)}, u32[]{:S(2)}, u32[]{:S(2)}) collective-permute-start(s32[1,1,128]{2,1,0:T(1,128)S(1)} %copy.83), channel_id=1, source_target_pairs={{0,32},{32,64},{64,96},{96,128},{128,160},{160,192},{192,224},{224... | collective-permute-start | bytes 1544 | tf_op jit(solution)/shard_map/while/body/eval_jaxpr/ppermute | solution.py:14
  113.4 12.4 %collective-permute-start = (bf16[1,2,128,256]{2,3,1,0:T(8,128)(2,1)S(1)}, bf16[1,2,128,256]{2,3,1,0:T(8,128)(2,1)S(1)}, u32[]{:S(2)}, u32[]{:S(2)}) collective-permute-start(bf16[1,2,128,256]{2,3,1,0:T(8,128)(2,1)S(1)} %copy.82), channel_id=1, source_target_pairs={{0,32},{32,64},{64,96},{96,128},{128,160},{160,192},{192,224},{224... | collective-permute-start | bytes 393224 | tf_op jit(solution)/shard_map/while/body/eval_jaxpr/ppermute | solution.py:14
  115.5 1.6 copy-start.1
  125.8 12.7 %collective-permute-start.1 = (s32[1,1,128]{2,1,0:T(1,128)S(1)}, s32[1,1,128]{2,1,0:T(1,128)S(1)}, u32[]{:S(2)}, u32[]{:S(2)}) collective-permute-start(s32[1,1,128]{2,1,0:T(1,128)S(1)} %copy.83), channel_id=1, source_target_pairs={{0,32},{32,64},{64,96},{96,128},{128,160},{160,192},{192,224},{224... | collective-permute-start | bytes 1544 | tf_op jit(solution)/shard_map/while/body/eval_jaxpr/ppermute | solution.py:14
  128.2 12.4 %collective-permute-start = (bf16[1,2,128,256]{2,3,1,0:T(8,128)(2,1)S(1)}, bf16[1,2,128,256]{2,3,1,0:T(8,128)(2,1)S(1)}, u32[]{:S(2)}, u32[]{:S(2)}) collective-permute-start(bf16[1,2,128,256]{2,3,1,0:T(8,128)(2,1)S(1)} %copy.82), channel_id=1, source_target_pairs={{0,32},{32,64},{64,96},{96,128},{128,160},{160,192},{192,224},{224... | collective-permute-start | bytes 393224 | tf_op jit(solution)/shard_map/while/body/eval_jaxpr/ppermute | solution.py:14
  130.3 1.6 copy-start.1
  140.6 12.7 %collective-permute-start.1 = (s32[1,1,128]{2,1,0:T(1,128)S(1)}, s32[1,1,128]{2,1,0:T(1,128)S(1)}, u32[]{:S(2)}, u32[]{:S(2)}) collective-permute-start(s32[1,1,128]{2,1,0:T(1,128)S(1)} %copy.83), channel_id=1, source_target_pairs={{0,32},{32,64},{64,96},{96,128},{128,160},{160,192},{192,224},{224... | collective-permute-start | bytes 1544 | tf_op jit(solution)/shard_map/while/body/eval_jaxpr/ppermute | solution.py:14
  143.1 12.4 %collective-permute-start = (bf16[1,2,128,256]{2,3,1,0:T(8,128)(2,1)S(1)}, bf16[1,2,128,256]{2,3,1,0:T(8,128)(2,1)S(1)}, u32[]{:S(2)}, u32[]{:S(2)}) collective-permute-start(bf16[1,2,128,256]{2,3,1,0:T(8,128)(2,1)S(1)} %copy.82), channel_id=1, source_target_pairs={{0,32},{32,64},{64,96},{96,128},{128,160},{160,192},{192,224},{224... | collective-permute-start | bytes 393224 | tf_op jit(solution)/shard_map/while/body/eval_jaxpr/ppermute | solution.py:14
  145.1 1.6 copy-start.1
  155.5 12.7 %collective-permute-start.1 = (s32[1,1,128]{2,1,0:T(1,128)S(1)}, s32[1,1,128]{2,1,0:T(1,128)S(1)}, u32[]{:S(2)}, u32[]{:S(2)}) collective-permute-start(s32[1,1,128]{2,1,0:T(1,128)S(1)} %copy.83), channel_id=1, source_target_pairs={{0,32},{32,64},{64,96},{96,128},{128,160},{160,192},{192,224},{224... | collective-permute-start | bytes 1544 | tf_op jit(solution)/shard_map/while/body/eval_jaxpr/ppermute | solution.py:14
  157.9 12.4 %collective-permute-start = (bf16[1,2,128,256]{2,3,1,0:T(8,128)(2,1)S(1)}, bf16[1,2,128,256]{2,3,1,0:T(8,128)(2,1)S(1)}, u32[]{:S(2)}, u32[]{:S(2)}) collective-permute-start(bf16[1,2,128,256]{2,3,1,0:T(8,128)(2,1)S(1)} %copy.82), channel_id=1, source_target_pairs={{0,32},{32,64},{64,96},{96,128},{128,160},{160,192},{192,224},{224... | collective-permute-start | bytes 393224 | tf_op jit(solution)/shard_map/while/body/eval_jaxpr/ppermute | solution.py:14
  170.3 12.7 %collective-permute-start.1 = (s32[1,1,128]{2,1,0:T(1,128)S(1)}, s32[1,1,128]{2,1,0:T(1,128)S(1)}, u32[]{:S(2)}, u32[]{:S(2)}) collective-permute-start(s32[1,1,128]{2,1,0:T(1,128)S(1)} %copy.83), channel_id=1, source_target_pairs={{0,32},{32,64},{64,96},{96,128},{128,160},{160,192},{192,224},{224... | collective-permute-start | bytes 1544 | tf_op jit(solution)/shard_map/while/body/eval_jaxpr/ppermute | solution.py:14
  172.7 12.4 %collective-permute-start = (bf16[1,2,128,256]{2,3,1,0:T(8,128)(2,1)S(1)}, bf16[1,2,128,256]{2,3,1,0:T(8,128)(2,1)S(1)}, u32[]{:S(2)}, u32[]{:S(2)}) collective-permute-start(bf16[1,2,128,256]{2,3,1,0:T(8,128)(2,1)S(1)} %copy.82), channel_id=1, source_target_pairs={{0,32},{32,64},{64,96},{96,128},{128,160},{160,192},{192,224},{224... | collective-permute-start | bytes 393224 | tf_op jit(solution)/shard_map/while/body/eval_jaxpr/ppermute | solution.py:14
  174.8 1.6 copy-start.1
  185.1 12.7 %collective-permute-start.1 = (s32[1,1,128]{2,1,0:T(1,128)S(1)}, s32[1,1,128]{2,1,0:T(1,128)S(1)}, u32[]{:S(2)}, u32[]{:S(2)}) collective-permute-start(s32[1,1,128]{2,1,0:T(1,128)S(1)} %copy.83), channel_id=1, source_target_pairs={{0,32},{32,64},{64,96},{96,128},{128,160},{160,192},{192,224},{224... | collective-permute-start | bytes 1544 | tf_op jit(solution)/shard_map/while/body/eval_jaxpr/ppermute | solution.py:14
  187.6 12.4 %collective-permute-start = (bf16[1,2,128,256]{2,3,1,0:T(8,128)(2,1)S(1)}, bf16[1,2,128,256]{2,3,1,0:T(8,128)(2,1)S(1)}, u32[]{:S(2)}, u32[]{:S(2)}) collective-permute-start(bf16[1,2,128,256]{2,3,1,0:T(8,128)(2,1)S(1)} %copy.82), channel_id=1, source_target_pairs={{0,32},{32,64},{64,96},{96,128},{128,160},{160,192},{192,224},{224... | collective-permute-start | bytes 393224 | tf_op jit(solution)/shard_map/while/body/eval_jaxpr/ppermute | solution.py:14
  199.9 12.7 %collective-permute-start.1 = (s32[1,1,128]{2,1,0:T(1,128)S(1)}, s32[1,1,128]{2,1,0:T(1,128)S(1)}, u32[]{:S(2)}, u32[]{:S(2)}) collective-permute-start(s32[1,1,128]{2,1,0:T(1,128)S(1)} %copy.83), channel_id=1, source_target_pairs={{0,32},{32,64},{64,96},{96,128},{128,160},{160,192},{192,224},{224... | collective-permute-start | bytes 1544 | tf_op jit(solution)/shard_map/while/body/eval_jaxpr/ppermute | solution.py:14
  202.4 12.4 %collective-permute-start = (bf16[1,2,128,256]{2,3,1,0:T(8,128)(2,1)S(1)}, bf16[1,2,128,256]{2,3,1,0:T(8,128)(2,1)S(1)}, u32[]{:S(2)}, u32[]{:S(2)}) collective-permute-start(bf16[1,2,128,256]{2,3,1,0:T(8,128)(2,1)S(1)} %copy.82), channel_id=1, source_target_pairs={{0,32},{32,64},{64,96},{96,128},{128,160},{160,192},{192,224},{224... | collective-permute-start | bytes 393224 | tf_op jit(solution)/shard_map/while/body/eval_jaxpr/ppermute | solution.py:14
  214.8 3.1 copy-start.3
  891.5 50.7 %all-to-all-start.3 = ((bf16[1,32,2,4096]{3,2,0,1:T(2,128)(2,1)}), bf16[1,32,2,4096]{3,2,0,1:T(2,128)(2,1)S(1)}, u32[]{:S(2)}, u32[]{:S(2)}) async-start(bf16[1,32,2,4096]{3,2,0,1:T(2,128)(2,1)} %reshape.64), calls=%async_computation.3 | async-start | bytes 1048576 | tf_op jit(solution)/shard_map/all_to_all | solution.py:109
  905.8 36.7 %copy-start.7 = (f32[1,128]{1,0:T(1,128)S(1)}, f32[1,128]{1,0:T(1,128)}, u32[]{:S(2)}) copy-start(f32[1,128]{1,0:T(1,128)} %param.13) | copy-start | bytes 1540
  (20 other events, 27.8 us)
Sparse Core Ops, SparseCore 0:
  683.6 132.4 all-gather.1
